TPU v7x, 256 devices: a whole 4x4x8 slice. The times are simulated.
256 devices in a mesh: wide: 32 (over z, y), narrow: 8 (over x, core).
Axes of the slice: x: 4, y: 4, z: 8, core: 2. Of those that a mesh axis runs over, the one named last changes fastest.
Arguments:
- values: bfloat16 [8192, 8192], P('wide', 'narrow'), as said below
- pattern: int32 [64, 64], P('wide', 'narrow'), may hold values from 0 to 1, as said below
- keep_mask: int32 [8192, 8192], P('wide', 'narrow'), may hold values 0 or 1
Outputs:
- clustered: float32 [8192, 8192], P('wide', 'narrow')
Inputs may be any that keep to these rules, and one draw needn't show every extreme that they name: Each device's block of tiles holds between 1 and 6 tiles with pattern 1, and some device's block holds exactly 6. `values`: entries lie in a positive range.
All inputs are finite; a program needn't handle non-finite values. No bound on the sum of `keep_mask` on one device may be relied on, other than what follows from the above.
Results may differ from a plain program's by a relative error of at most 0.0003.
Values may be sent and summed in bfloat16 or wider, within the bound.
A program may use at most 256 MiB of HBM per device.

v0:
```python
import functools
import heapq

import jax
import jax.numpy as jnp
from jax import lax
from jax.experimental import pallas as pl
from jax.experimental.pallas import tpu as pltpu
from jax.sharding import PartitionSpec as P

TILE = 128
KEEP = 6
SLOTS = KEEP + 2
UNIT = 32
PART = TILE // UNIT
PACKED = KEEP * PART
NZ, NY, NX, NC = 8, 4, 4, 2
RETIRE = 20
LEADS = (0.5, 2.5)
Z_UNITS = 14
MESH = pl.DeviceIdType.MESH


def ring_hops(n):
    full = (n - 1) // 2
    hops = []
    for step in (1, -1):
        for hop in range(full):
            hops.append(((-step * hop) % n, (-step * (hop + 1)) % n, step, None))
        if n % 2 == 0:
            half = 0 if step == 1 else 1
            hops.append(((-step * full) % n, (-step * (full + 1)) % n, step, half))
    return hops


def block_transfers():
    def rows(part, half):
        low, high = (0, Z_UNITS) if part == "z" else (Z_UNITS, PACKED)
        middle = (low + high) // 2
        return ((low, high), (low, middle), (middle, high))[0 if half is None else half + 1]

    found = []
    for a, b, step, half in ring_hops(NZ):
        found.append(("z", "z", step, (0, a), (0, b), rows("z", half)))
    for a, b, step, half in ring_hops(NY):
        found.append(("y", "y", step, (a, 0), (b, 0), rows("y", half)))
    for dz in range(NZ):
        for a, b, step, half in ring_hops(NY):
            found.append(("z", "y", step, (a, dz), (b, dz), rows("z", half)))
    for dy in range(NY):
        for a, b, step, half in ring_hops(NZ):
            found.append(("y", "z", step, (dy, a), (dy, b), rows("y", half)))
    return found


def plan(transfers, lead, rate=60e3, latency=2.5):
    have = {("z", 0, 0): [(0, Z_UNITS)], ("y", 0, 0): [(Z_UNITS, PACKED)]}
    waiting = list(range(len(transfers)))
    queues, free, events = {}, {}, []
    arrivals, starts, cause_of = [], {}, {}

    def ready(index):
        part, _, _, (dy, dz), _, (low, high) = transfers[index]
        for a, b in sorted(have.get((part, dy, dz), [])):
            if a <= low < b:
                low = b
        return low >= high

    def pump(now, cause):
        for index in [i for i in waiting if ready(i)]:
            waiting.remove(index)
            queues.setdefault(transfers[index][1:3], []).append(index)
            cause_of[index] = cause
        for link, queue in queues.items():
            if queue and free.get(link, 0.0) <= now:
                queue.sort(key=lambda i: (transfers[i][0] != link[0], i))
                index = queue.pop(0)
                low, high = transfers[index][5]
                took = (high - low) * UNIT * TILE * 2 / rate
                free[link] = now + took
                starts[index] = now
                heapq.heappush(events, (now + took, -1))
                heapq.heappush(events, (now + took + latency, index))

    pump(0.0, -1)
    while events:
        now, index = heapq.heappop(events)
        if index >= 0:
            part, _, _, _, (dy, dz), rows = transfers[index]
            have.setdefault((part, dy, dz), []).append(rows)
            arrivals.append((now, index))
        pump(now, index)
    arrived_at = {index: now for now, index in arrivals}
    released = {-1: []}
    for index in sorted(starts, key=lambda i: (starts[i], i)):
        cause = cause_of[index]
        for now, earlier in arrivals:
            if now > starts[index] - lead:
                break
            if cause == -1 or now > arrived_at[cause]:
                cause = earlier
        released.setdefault(cause, []).append(index)
    return arrivals, released


def kernel(
    col_tiles,
    pattern,
    values,
    keep,
    out,
    held,
    last,
    slab,
    dense,
    keep_v,
    pattern_s,
    values_v,
    tiles,
    meta_b,
    meta_a,
    meta_v,
    meta_s,
    tot_y,
    tot_z,
    send_sem,
    recv_sem,
    side_send,
    side_recv,
    small_send,
    small_recv,
    local_sem,
):
    wide, narrow = lax.axis_index("wide"), lax.axis_index("narrow")
    z, y = wide // NY, wide % NY
    x, core = narrow // NC, narrow % NC
    blocks = NX * NC

    def at(dy=0, dz=0):
        return (lax.rem(z + dz, NZ) * NY + lax.rem(y + dy, NY), narrow)

    def beside(dx, dc):
        return (wide, lax.rem(x + dx, NX) * NC + lax.rem(core + dc, NC))

    def remote(src, dst, send, recv, device):
        return pltpu.make_async_remote_copy(
            src_ref=src, dst_ref=dst, send_sem=send, recv_sem=recv, device_id=device, device_id_type=MESH
        )

    pattern_copy = pltpu.make_async_copy(pattern, pattern_s, local_sem.at[1])
    pattern_copy.start()
    values_copy = pltpu.make_async_copy(values, values_v, local_sem.at[2])
    values_copy.start()
    z_peers = list(range(1, NZ))
    y_peers = list(range(1, NY))
    x_peers = list(range(1, NX))
    peers = [at(dz=d) for d in z_peers] + [at(dy=d) for d in y_peers] + [beside(d, 0) for d in x_peers]
    sibling = beside(0, 1)
    barrier = pltpu.get_barrier_semaphore()
    for peer in peers:
        pl.semaphore_signal(barrier, inc=1, device_id=peer, device_id_type=MESH)

    @pl.when(core == 0)
    def _():
        pl.semaphore_signal(barrier, inc=1, device_id=sibling, device_id_type=MESH)

    eye = (
        lax.broadcasted_iota(jnp.int32, (TILE, TILE), 0) == lax.broadcasted_iota(jnp.int32, (TILE, TILE), 1)
    ).astype(jnp.float32)
    lane = lax.broadcasted_iota(jnp.int32, (8, TILE), 1)
    def same(a, b):
        return jnp.maximum(0, 1 - jnp.maximum(a - b, b - a))

    zero = jnp.int32(0)
    filled = zero
    picked = [zero] * KEEP
    pattern_copy.wait()
    codes = jnp.zeros((8, TILE), jnp.int32)
    for r in range(2):
        for c in range(col_tiles):
            present = pattern_s[r, c]
            diagonal = jnp.where(2 * wide + r == col_tiles * narrow + c, 1, 0)
            code = present * filled + (1 - present) * (KEEP + diagonal)
            codes = jnp.where(lane == r * col_tiles + c, code, codes)
            for s in range(KEEP):
                mine = present * same(filled, s)
                picked[s] += mine * (r * col_tiles + c)
            filled = filled + present
    shift = 2 * TILE * wide - col_tiles * TILE * narrow
    corner = 2 * wide - col_tiles * narrow
    values_copy.wait()
    for r in range(2):
        for c in range(col_tiles):
            tiles[r * col_tiles + c] = values_v[r * TILE : (r + 1) * TILE, c * TILE : (c + 1) * TILE]
    for s, position in enumerate(picked):
        on = same(position, corner) + same(position, corner + 1 + col_tiles)
        inside = jnp.where(jnp.logical_and(corner >= 0, corner < col_tiles), 1, 0)
        on = (on * inside).astype(jnp.float32)
        tile = (tiles[position].astype(jnp.float32) + on * eye).astype(jnp.bfloat16)
        tile = tile.reshape(PART, UNIT, TILE)
        slab[narrow, s * PART : (s + 1) * PART] = tile
        held[0][y, s * PART : (s + 1) * PART] = tile
    meta_b[0, 0] = codes
    meta_a[core, x] = codes

    pl.semaphore_wait(barrier, len(peers) + core)

    transfers = block_transfers()
    arrivals, _ = plan(transfers, LEADS[0])
    released = [plan(transfers, lead)[1] for lead in LEADS]
    final = transfers[arrivals[-1][1]][4][1]

    def place(dy, dz):
        return last[dy].at[0] if dz == final else held[dz].at[lax.rem(y + dy, NY)]


    def block_copy(index):
        _, axis, step, there, here, (low, high) = transfers[index]
        device = at(dz=step % NZ) if axis == "z" else at(dy=step % NY)
        window = pl.ds(low, high - low)
        if here[1] == final:
            target = last[here[0]].at[0]
        else:
            target = held[here[1]].at[lax.rem(y + there[0], NY)]
        return remote(
            place(*there).at[window], target.at[window], send_sem.at[index], recv_sem.at[index], device
        )

    def block_arrival(index):
        _, axis, step, _, (dy, dz), (low, high) = transfers[index]
        device = at(dz=step % NZ) if axis == "z" else at(dy=step % NY)
        here = place(dy, dz).at[pl.ds(low, high - low)]
        return remote(here, here, send_sem.at[index], recv_sem.at[index], device)

    sent = []

    def start(copy):
        copy.start()
        sent.append(copy)

    half_started = set()

    def start_after(event):
        first, second = (plan_.get(event, []) for plan_ in released)
        for index in first:
            if index in second:
                start(block_copy(index))
        for which, some, others in ((0, first, second), (1, second, first)):
            for index in some:
                if index in others:
                    continue
                copy = block_copy(index)
                pl.when(core == which)(copy.start)
                if index in half_started:
                    sent.append(copy)
                half_started.add(index)

    start_after(-1)

    def side_copy(index, block, device):
        ref = slab.at[block, pl.ds(0, PACKED)]
        return remote(ref, ref, side_send.at[index], side_recv.at[index], device)

    own_to_sibling = side_copy(0, narrow, sibling)
    for dx in x_peers:
        start(side_copy(dx, narrow, beside(dx, 0)))
    pl.when(core == 1)(own_to_sibling.start)

    for k, d in enumerate(z_peers):
        start(remote(meta_b.at[0, 0], meta_b.at[0, NZ - d], small_send.at[k], small_recv.at[k], at(dz=d)))
    first_x = len(z_peers)
    for k, dx in enumerate(x_peers):
        k += first_x
        own = meta_a.at[core, x]
        start(remote(own, own, small_send.at[k], small_recv.at[k], beside(dx, 0)))
    first_sibling = first_x + len(x_peers)
    first_y = first_sibling + 1
    first_total = first_y + len(y_peers)

    keep_copy = pltpu.make_async_copy(keep, keep_v, local_sem.at[0])
    keep_copy.start()
    blank = jnp.zeros((PART, UNIT, TILE), jnp.bfloat16)
    unit = eye.astype(jnp.bfloat16).reshape(PART, UNIT, TILE)
    for ref, count in [(slab, blocks)] + [(held[dz], NY) for dz in range(NZ) if dz != final] + [(ref, 1) for ref in last]:
        for i in range(count):
            ref[i, PACKED : PACKED + PART] = blank
            ref[i, PACKED + PART : PACKED + 2 * PART] = unit

    def meta_along_y():
        for k, d in enumerate(z_peers):
            here = meta_b.at[0, NZ - d]
            remote(here, here, small_send.at[k], small_recv.at[k], at(dz=d)).wait_recv()
        for k, d in enumerate(y_peers):
            k += first_y
            start(remote(meta_b.at[0], meta_b.at[NY - d], small_send.at[k], small_recv.at[k], at(dy=d)))

    def meta_to_scalars():
        theirs = meta_a.at[1 - core]
        remote(theirs, theirs, small_send.at[first_sibling], small_recv.at[first_sibling], sibling).wait_recv()
        for k, d in enumerate(y_peers):
            k += first_y
            here = meta_b.at[NY - d]
            remote(here, here, small_send.at[k], small_recv.at[k], at(dy=d)).wait_recv()
        for dz in range(NZ):
            for dy in range(NY):
                row = dz * NY + dy
                meta_v[row : row + 1, :] = meta_b[dy, dz, 0:1, :]
        for n in range(blocks):
            row = NZ * NY + n
            meta_v[row : row + 1, :] = meta_a[n % NC, n // NC, 0:1, :]
        copy = pltpu.make_async_copy(meta_v, meta_s, local_sem.at[3])
        copy.start()
        copy.wait()

    def side_arrivals():
        @pl.when(core == 0)
        def _():
            side_copy(0, narrow + 1, sibling).wait_recv()
            own_to_sibling.start()

        for k, dx in enumerate(x_peers):
            source = lax.rem(x + NX - dx, NX) * NC + core
            side_copy(dx, source, beside(dx, 0)).wait_recv()
            start(side_copy(NX - 1 + dx, source, sibling))
            k += first_x
            here = meta_a.at[core, lax.rem(x + NX - dx, NX)]
            remote(here, here, small_send.at[k], small_recv.at[k], beside(dx, 0)).wait_recv()
        ours = meta_a.at[core]
        start(remote(ours, ours, small_send.at[first_sibling], small_recv.at[first_sibling], sibling))
        sent.append(own_to_sibling)

    def tile_of(ref, block, code):
        return ref[block, pl.ds(code * PART, PART)].reshape(TILE, TILE)

    def expand_slab():
        @pl.when(core == 1)
        def _():
            side_copy(0, narrow - 1, sibling).wait_recv()

        for dx in x_peers:
            source = lax.rem(x + NX - dx, NX) * NC + 1 - core
            side_copy(NX - 1 + dx, source, sibling).wait_recv()

        def body(n, carry):
            for r in range(2):
                for c in range(col_tiles):
                    code = meta_s[NZ * NY + n, r * col_tiles + c]
                    dense[n, r * TILE : (r + 1) * TILE, c * TILE : (c + 1) * TILE] = tile_of(slab, n, code)
            return carry

        lax.fori_loop(0, blocks, body, 0)

    row_id = lax.broadcasted_iota(jnp.int32, (2 * TILE, TILE), 0)
    col_id = lax.broadcasted_iota(jnp.int32, (2 * TILE, TILE), 1)

    def strip(ref, row, dy, dz, pair):
        halves = []
        for r in range(2):
            codes = [meta_s[dz * NY + dy, r * col_tiles + pair * 2 + c] for c in range(2)]
            halves.append(jnp.concatenate([tile_of(ref, row, code) for code in codes], axis=1))
        return halves

    def multiply_plane(dz, pair, first):
        halves = []
        for row in range(NY):
            halves += strip(held[dz], row, lax.rem(row - y + NY, NY), dz, pair)
        product = jnp.dot(
            dense[lax.rem(z + dz, NZ)], jnp.concatenate(halves, axis=0), preferred_element_type=jnp.float32
        )
        columns = slice(pair * 2 * TILE, (pair + 1) * 2 * TILE)
        if first:
            out[:, columns] = product
        else:
            out[:, columns] += product

    def multiply_block(dy, pair, finish):
        depth = pl.ds(pl.multiple_of(lax.rem(y + dy, NY) * 2 * TILE, 2 * TILE), 2 * TILE)
        rhs = jnp.concatenate(strip(last[dy], 0, dy, final, pair), axis=0)
        product = jnp.dot(dense[lax.rem(z + final, NZ), :, depth], rhs, preferred_element_type=jnp.float32)
        columns = slice(pair * 2 * TILE, (pair + 1) * 2 * TILE)
        if not finish:
            out[:, columns] += product
            return
        product = out[:, columns] + product
        for half in range(2):
            c = pair * 2 + half
            columns = slice(c * TILE, (c + 1) * TILE)
            value = product[:, half * TILE : (half + 1) * TILE]
            kept = jnp.logical_or(keep_v[:, columns] == 1, row_id + shift == col_id + c * TILE)
            pruned = jnp.where(kept, value * value, 0.0)
            out[:, columns] = pruned
            tot_y[0, c : c + 1, :] = jnp.sum(pruned, axis=0, keepdims=True)

    extras = [(9.0, meta_along_y), (17.0, side_arrivals), (18.0, meta_to_scalars), (21.0, expand_slab)]
    pairs = col_tiles // 2
    left = {}

    def unit_of(index):
        dy, dz = transfers[index][4]
        return (dy, dz) if dz == final else (None, dz)

    for _, index in arrivals:
        left[unit_of(index)] = left.get(unit_of(index), 0) + 1
    blocks_left = NY
    queue, multiplied = [], []
    issued, settled = [], 0
    clock = 0.0

    def run(budget):
        nonlocal clock
        while queue and extras == [] and clock + queue[0][0] <= budget:
            cost, action = queue.pop(0)
            action()
            clock += cost

    for now, index in arrivals:
        end = index == arrivals[-1][1]
        while extras and (end or extras[0][0] <= now):
            extras.pop(0)[1]()
        run(float("inf") if end else now)
        block_arrival(index).wait_recv()
        clock = max(clock, now)
        start_after(index)
        issued.append(len(sent))
        while len(issued) > RETIRE and settled < issued[-RETIRE]:
            sent[settled].wait_send()
            settled += 1
        left[unit_of(index)] -= 1
        if left[unit_of(index)] == 0:
            dy, dz = unit_of(index)
            for pair in range(pairs):
                if dy is None:
                    queue.append((0.3, functools.partial(multiply_plane, dz, pair, not multiplied)))
                else:
                    queue.append((0.1, functools.partial(multiply_block, dy, pair, blocks_left == 1)))
            if dy is None:
                multiplied.append(dz)
            else:
                blocks_left -= 1
    keep_copy.wait()
    if col_tiles < 8:
        tot_y[0] = jnp.ones((8, TILE), jnp.float32)
    run(float("inf"))

    for k, d in enumerate(y_peers):
        k += first_total
        start(remote(tot_y.at[0], tot_y.at[NY - d], small_send.at[k], small_recv.at[k], at(dy=d)))
    before = len(sent) - len(y_peers)
    for copy in sent[settled:before]:
        copy.wait_send()
    for k, d in enumerate(y_peers):
        k += first_total
        here = tot_y.at[NY - d]
        remote(here, here, small_send.at[k], small_recv.at[k], at(dy=d)).wait_recv()
    tot_z[0] = functools.reduce(jnp.add, [tot_y[d] for d in range(NY)])
    first_total_z = first_total + len(y_peers)
    for k, d in enumerate(z_peers):
        k += first_total_z
        start(remote(tot_z.at[0], tot_z.at[NZ - d], small_send.at[k], small_recv.at[k], at(dz=d)))
    for k, d in enumerate(z_peers):
        k += first_total_z
        here = tot_z.at[NZ - d]
        remote(here, here, small_send.at[k], small_recv.at[k], at(dz=d)).wait_recv()
    total = functools.reduce(jnp.add, [tot_z[d] for d in range(NZ)])
    scale = (2 * TILE * NZ * NY) / total
    for c in range(col_tiles):
        columns = slice(c * TILE, (c + 1) * TILE)
        out[:, columns] = out[:, columns] * scale[c : c + 1, :]
    for copy in sent[before:]:
        copy.wait_send()


def shards(values, pattern, keep_mask):
    rows, cols = values.shape
    col_tiles = cols // TILE
    blocks = NX * NC
    transfers = len(block_transfers())
    small = 2 * (NZ - 1) + 2 * (NY - 1) + NX
    return pl.pallas_call(
        functools.partial(kernel, col_tiles),
        out_shape=jax.ShapeDtypeStruct((rows, cols), jnp.float32),
        in_specs=[
            pl.BlockSpec(memory_space=pltpu.HBM),
            pl.BlockSpec(memory_space=pltpu.HBM),
            pl.BlockSpec(memory_space=pltpu.HBM),
        ],
        out_specs=pl.BlockSpec(memory_space=pltpu.VMEM),
        scratch_shapes=[
            [pltpu.VMEM((NY, SLOTS * PART, UNIT, TILE), jnp.bfloat16) for _ in range(NZ)],
            [pltpu.VMEM((1, SLOTS * PART, UNIT, TILE), jnp.bfloat16) for _ in range(NY)],
            pltpu.VMEM((blocks, SLOTS * PART, UNIT, TILE), jnp.bfloat16),
            pltpu.VMEM((blocks, rows, cols), jnp.bfloat16),
            pltpu.VMEM((rows, cols), jnp.int32),
            pltpu.SMEM((2, col_tiles), jnp.int32),
            pltpu.VMEM((rows, cols), jnp.bfloat16),
            pltpu.VMEM((2 * col_tiles, TILE, TILE), jnp.bfloat16),
            pltpu.VMEM((NY, NZ, 8, TILE), jnp.int32),
            pltpu.VMEM((NC, NX, 8, TILE), jnp.int32),
            pltpu.VMEM((NZ * NY + blocks, TILE), jnp.int32),
            pltpu.SMEM((NZ * NY + blocks, TILE), jnp.int32),
            pltpu.VMEM((NY, 8, TILE), jnp.float32),
            pltpu.VMEM((NZ, 8, TILE), jnp.float32),
            pltpu.SemaphoreType.DMA((transfers,)),
            pltpu.SemaphoreType.DMA((transfers,)),
            pltpu.SemaphoreType.DMA((2 * NX - 1,)),
            pltpu.SemaphoreType.DMA((2 * NX - 1,)),
            pltpu.SemaphoreType.DMA((small,)),
            pltpu.SemaphoreType.DMA((small,)),
            pltpu.SemaphoreType.DMA((4,)),
        ],
        compiler_params=pltpu.CompilerParams(
            collective_id=0, has_side_effects=True, vmem_limit_bytes=52 * 1024 * 1024
        ),
        cost_estimate=pl.CostEstimate(flops=2 * rows * cols * 8192, bytes_accessed=12 << 20, transcendentals=0),
    )(*[pltpu.with_memory_space_constraint(operand, pltpu.HBM) for operand in (pattern, values, keep_mask)])


def solution(mesh):
    return jax.shard_map(
        shards,
        mesh=mesh,
        in_specs=(P("wide", "narrow"), P("wide", "narrow"), P("wide", "narrow")),
        out_specs=P("wide", "narrow"),
        check_vma=False,
    )
```

profile of v0, /device:TPU:2, one launch (start us, length us, event | category | flops | bytes accessed | tf_op | source)
XLA Modules:
  0.0 59.2 jit_solution(11010504781307088652)
XLA Ops:
  0.0 58.3 %shard_map.37 = f32[256,1024]{1,0:T(8,128)S(1)} custom-call(s32[2,8]{1,0:T(2,128)} %pattern.1, bf16[256,1024]{1,0:T(8,128)(2,1)} %values.1, s32[256,1024]{1,0:T(8,128)} %keep.1), custom_call_target="tpu_custom_call" | custom-call | flops 4294967296 | bytes 12582912 | tf_op jit(solution)/shard_map/pallas_call | solution.py:479
  58.3 1.0 %copy.5 = f32[256,1024]{1,0:T(8,128)} copy(f32[256,1024]{1,0:T(8,128)S(1)} %shard_map.37) | data formatting | bytes 2097152
where the time goes:
time: 59.4 us; the launch traced here: 59.2 us
  Pallas kernels  58.3 us (98%)
  local copies, waits for them, and re-layouts  0.97 us (2%)
    pallas_call x1, Pallas kernels, shards(): pl.pallas_call(functools.partial(kernel, col_tiles), out_shape=jax.ShapeD...  58.3 us

commit v1 on v0

--- a/solution.py
+++ b/solution.py
@@ -53,7 +53,7 @@
     return found
 
 
-def plan(transfers, lead, rate=60e3, latency=2.5):
+def plan(transfers, lead, rate=60e3, latency=3.0):
     have = {("z", 0, 0): [(0, Z_UNITS)], ("y", 0, 0): [(Z_UNITS, PACKED)]}
     waiting = list(range(len(transfers)))
     queues, free, events = {}, {}, []

time: 59.4 us -> 58.9 us (level)
  no operation moved by 1% of the time
where the time goes in v1:
time: 58.9 us
  Pallas kernels  57.9 us (98%)
  local copies, waits for them, and re-layouts  0.97 us (2%)
    pallas_call x1, Pallas kernels, shards(): pl.pallas_call(functools.partial(kernel, col_tiles), out_shape=jax.ShapeD...  57.9 us

profile of v1, /device:TPU:2, one launch (start us, length us, event | category | flops | bytes accessed | tf_op | source)
XLA Modules:
  0.0 58.9 jit_solution(6921539710409184024)
XLA Ops:
  0.0 57.9 %shard_map.37 = f32[256,1024]{1,0:T(8,128)S(1)} custom-call(s32[2,8]{1,0:T(2,128)} %pattern.1, bf16[256,1024]{1,0:T(8,128)(2,1)} %values.1, s32[256,1024]{1,0:T(8,128)} %keep.1), custom_call_target="tpu_custom_call" | custom-call | flops 4294967296 | bytes 12582912 | tf_op jit(solution)/shard_map/pallas_call | solution.py:479
  57.9 1.0 %copy.5 = f32[256,1024]{1,0:T(8,128)} copy(f32[256,1024]{1,0:T(8,128)S(1)} %shard_map.37) | data formatting | bytes 2097152
